TPU v7x, 32 devices: a whole 2x2x4 slice. The times are simulated.
32 devices in a mesh: groups: 2 (over y), seq: 4 (over z), dp: 2 (over x), strand: 2 (over core).
Axes of the slice: x: 2, y: 2, z: 4, core: 2. Of those that a mesh axis runs over, the one named last changes fastest.
Arguments:
- tokens: int32 [4, 2048], P(('groups', 'dp'), 'seq'), parts along dimension 0, may hold values from 0 to 3
- stem_table: bfloat16 [15, 4, 1536], replicated, may hold values from -1.5 to 1.5
- conv_weight: bfloat16 [3, 1536, 768], P(None, 'dp'), may hold values from -0.09375 to 0.09375
- gain_in: float32 [1536], replicated, may hold values from 0.1 to 1.9
- gain_mid: float32 [768], replicated, may hold values from 0.1 to 1.9
- point_weight: bfloat16 [768, 1536], P('dp'), may hold values from -0.21875 to 0.21875
Outputs:
- embedding: bfloat16 [4, 2048, 1536], P(('groups', 'dp'), 'seq', 'strand'), parts along dimension 0
There are 2 independent parts, one for each index of `groups`. A program takes and returns all parts, laid end to end along the dimension named above; an argument that names none is the same for every part. Nothing has to cross between parts.
All inputs are finite; a program needn't handle non-finite values.
Results may differ from a plain program's by a relative error of at most 0.009.
Values may be sent and summed in bfloat16 or wider, within the bound.
No kernel may reach another device: no remote copies, remote signals or barrier semaphores. Data moves between devices by JAX's collectives and lax.ppermute only.
A program may use at most 64 MiB of HBM per device.

v0:
```python
import functools

import jax
import jax.numpy as jnp
from jax import lax
from jax.experimental import pallas as pl
from jax.experimental.pallas import tpu as pltpu
from jax.sharding import PartitionSpec as P

DILATION = 256
EPS = 1e-06
ROW_STEP = 128
CHUNKS = ((0, 64), (64, 128), (192, 64))
TAILS = ((0, 1), (2,))
KINDS = 4
FLOPS = {
    "early": 0.1,
    "sent0": 5.0,
    "sent1": 15.0,
    "sent2": 0.5,
    "own": 15.0,
    "middle0": 5.0,
    "middle1": 5.0,
    "final0": 2.0,
    "final1": 5.0,
}
MIB = 2**20


def ring_pairs(axis, distance):
    count = lax.axis_size(axis)
    return [(i, (i + distance) % count) for i in range(count)]


def base_taps(tok_ref, step, row_count):
    count, blocks = lax.axis_size("dp"), lax.axis_size("seq")
    here = lax.axis_index("seq")
    first = lax.rem(lax.axis_index("dp") + step, count) * blocks
    sides = [jnp.maximum(here - 1, 0), here, jnp.minimum(here + 1, blocks - 1)]
    bases = jnp.concatenate([tok_ref[first + side] for side in sides], axis=1)
    width, span = 3 * row_count, row_count + 2 * DILATION
    spread = jnp.broadcast_to(bases, (16, width))
    start = width - (row_count - DILATION + 8)
    taps = pltpu.roll(spread, start, 1, stride=1, stride_axis=0)[:, :span]
    place = lax.broadcasted_iota(jnp.int32, (16, span), 1) + (here * row_count - DILATION)
    source = place + 8 - lax.broadcasted_iota(jnp.int32, (16, span), 0)
    length = blocks * row_count
    inside = (place >= 0) & (place < length) & (source >= 0) & (source < length)
    return jnp.where(inside, taps, -1).astype(jnp.float32).astype(jnp.bfloat16)


def one_hot(taps, second, table_rows):
    row = lax.broadcasted_iota(jnp.int32, (table_rows, 16), 0) // KINDS
    column = lax.broadcasted_iota(jnp.int32, (table_rows, 16), 1)
    chosen = (column == 15 - row + second * (2 * row - 14)).astype(jnp.float32)
    values = jnp.dot(chosen.astype(jnp.bfloat16), taps, preferred_element_type=jnp.float32)
    base = lax.broadcasted_iota(jnp.int32, values.shape, 0) % KINDS
    base = base + second * (KINDS - 1 - 2 * base)
    return (values == base.astype(jnp.float32)).astype(jnp.float32).T


def gelu(x):
    inner = x * (0.7978845608028654 + 0.035677408136300125 * (x * x))
    half = 0.5 * x
    return half + half * jnp.tanh(inner)


def activate(hot, table_ref, gain_ref, act_ref):
    depth = gain_ref.shape[1]
    for start in range(0, hot.shape[0], ROW_STEP):
        embedded = jnp.dot(
            hot[start : start + ROW_STEP], table_ref[...], preferred_element_type=jnp.float32
        )
        mean = jnp.mean(embedded * embedded, axis=-1, keepdims=True)
        scaled = embedded[:, :depth] * lax.rsqrt(mean + EPS) * gain_ref[...]
        act_ref[start : start + ROW_STEP] = gelu(scaled).astype(jnp.bfloat16)


def convolve(blocks, w_ref):
    second = lax.axis_index("strand")
    total = None
    for tap, block in enumerate(blocks):
        weight = w_ref[tap + second * (2 - 2 * tap)]
        part = jnp.dot(block, weight, preferred_element_type=jnp.float32)
        total = part if total is None else total + part
    return total


def send_kernel(tok_any, point_any, spread_ref, piece_ref, tok_ref, sems):
    rows, columns = piece_ref.shape
    low = pl.multiple_of(lax.axis_index("groups") * rows, 16)
    left = pl.multiple_of(lax.axis_index("strand") * columns, 128)
    part = point_any.at[pl.ds(low, rows), pl.ds(left, columns)]
    copies = [
        pltpu.make_async_copy(tok_any, tok_ref, sems.at[0]),
        pltpu.make_async_copy(part, piece_ref, sems.at[1]),
    ]
    for copy in copies:
        copy.start()
    copies[0].wait()
    spread_ref[...] = jnp.broadcast_to(tok_ref[...][None], spread_ref.shape)
    copies[1].wait()


def load_kernel(stem_any, gain_any, w_any, table_ref, plain_ref, gain_here_ref, w_ref, *scratch):
    stem_ref, gain_ref, flat_ref, sems = scratch
    depth = w_any.shape[1]
    copies = [
        pltpu.make_async_copy(stem_any, stem_ref, sems.at[0]),
        pltpu.make_async_copy(gain_any, gain_ref, sems.at[1]),
    ]
    for index, (tap, low, rows) in enumerate(weight_parts(w_any)):
        part = (tap, pl.ds(low, rows))
        copies.append(pltpu.make_async_copy(w_any.at[part], w_ref.at[part], sems.at[index + 2]))
    for copy in copies:
        copy.start()
    copies[0].wait()
    taps, kinds, width = stem_ref.shape
    slabs = [stem_ref[tap].astype(jnp.float32) for tap in range(taps)]
    slabs += [jnp.zeros((kinds, width), jnp.float32)] * (16 - taps)
    flat = jnp.concatenate(slabs)
    flat_ref[...] = flat.astype(jnp.bfloat16)
    left = lax.axis_index("dp") * depth
    turn = lax.rem(width - left, width)
    table_ref[...] = pltpu.roll(flat, turn, 1).astype(jnp.bfloat16)
    copies[1].wait()
    gain = jnp.broadcast_to(gain_ref[...].reshape(1, width), (8, width))
    gain_here_ref[...] = pltpu.roll(gain, turn, 1)[:1, :depth]
    half = plain_ref.shape[1]
    column = pl.multiple_of(lax.axis_index("strand") * half, 128)
    plain_ref[...] = flat_ref[:, pl.ds(column, half)]
    for copy in copies[2:]:
        copy.wait()


def weight_parts(weight):
    rows = weight.shape[1] // 2
    return [(tap, low, rows) for tap in range(weight.shape[0]) for low in (0, rows)]


def chunk_kernel(step, low, size, row_count, out_index, *refs):
    tok_ref, table_ref, gain_ref, w_ref = refs[:4]
    out_ref, act_ref = refs[out_index], refs[-1]
    taps = base_taps(tok_ref, step, row_count)
    hot = one_hot(taps, lax.axis_index("strand"), table_ref.shape[0])
    blocks = row_count // DILATION
    pieces = [hot[b * DILATION + low :][:size] for b in range(blocks + 2)]
    activate(jnp.concatenate(pieces).astype(jnp.bfloat16), table_ref, gain_ref, act_ref)
    parts = [act_ref[t * size : (t + blocks) * size] for t in range(3)]
    out_ref[...] = convolve(parts, w_ref).astype(jnp.bfloat16)


def rows_of(ref, low, size):
    starts = range(low, ref.shape[0], DILATION)
    return jnp.concatenate([ref[start : start + size] for start in starts])


def middle_of(own_ref, gain_ref, parts, low, size):
    total = rows_of(own_ref, low, size)
    for ref in parts:
        total = total + ref[...].astype(jnp.float32)
    mean = jnp.mean(total * total, axis=-1, keepdims=True)
    return gelu(total * lax.rsqrt(mean + EPS) * gain_ref[...].reshape(1, -1)).astype(
        jnp.bfloat16
    )


def own_kernel(places, piece_rows, *refs):
    tok_ref, table_ref, plain_ref, gain_ref, w_ref = refs[:5]
    pieces = refs[6 : 6 + len(places)]
    out_ref, res_ref, point_ref, act_ref, sems = refs[6 + len(places) :]
    ranks, groups = lax.axis_size("dp"), lax.axis_size("groups")
    me, group = lax.axis_index("dp"), lax.axis_index("groups")
    copies = []
    for index, (step, turn) in enumerate(places):
        place = lax.rem(me + step, ranks) * (piece_rows * groups)
        if step:
            place = place + lax.rem(group + turn, groups) * piece_rows
        source = pieces[index]
        if not step:
            columns = point_ref.shape[1]
            left = pl.multiple_of(lax.axis_index("strand") * columns, 128)
            source = source.at[:, pl.ds(left, columns)]
        target = pl.ds(pl.multiple_of(place, 16), source.shape[0])
        copies.append(pltpu.make_async_copy(source, point_ref.at[target], sems.at[index]))
        copies[-1].start()
    row_count = out_ref.shape[0]
    second = lax.axis_index("strand")
    taps = base_taps(tok_ref, 0, row_count)
    hot = one_hot(taps, second, table_ref.shape[0])
    here = slice(DILATION, DILATION + row_count)
    both = hot[here] + one_hot(taps[:, here], 1 - second, table_ref.shape[0])
    res_ref[...] = jnp.dot(
        both.astype(jnp.bfloat16), plain_ref[...], preferred_element_type=jnp.float32
    )
    activate(hot.astype(jnp.bfloat16), table_ref, gain_ref, act_ref)
    blocks = [act_ref[t * DILATION : t * DILATION + row_count] for t in range(3)]
    out_ref[...] = convolve(blocks, w_ref)
    for copy in copies:
        copy.wait()


def middle_kernel(chunks, count, own_ref, gain_ref, *refs):
    out_ref = refs[-1]
    first, total_size = chunks[0][0], sum(size for _, size in chunks)
    for index, (low, size) in enumerate(chunks):
        parts = refs[index * count : (index + 1) * count]
        value = middle_of(own_ref, gain_ref, parts, low, size)
        for block in range(own_ref.shape[0] // DILATION):
            start = block * total_size + low - first
            out_ref[start : start + size] = value[block * size : (block + 1) * size]


def final_kernel(low, size, mine_ref, other_ref, res_ref, point_ref, *refs):
    out_ref = refs[-1]
    total = mine_ref[...].astype(jnp.float32) + other_ref[...].astype(jnp.float32)
    branch = jnp.dot(
        total.astype(jnp.bfloat16), point_ref[...], preferred_element_type=jnp.float32
    )
    value = (0.5 * (branch + rows_of(res_ref, low, size))).astype(jnp.bfloat16)
    out_ref[...] = value.reshape(out_ref.shape)


def pinned(x):
    return pltpu.with_memory_space_constraint(x, pltpu.VMEM)


def in_hbm(x):
    return pltpu.with_memory_space_constraint(x, pltpu.HBM)


def cost(kind):
    return pl.CostEstimate(
        flops=int(1e9 * FLOPS[kind]), bytes_accessed=2**20, transcendentals=0
    )


def per_device(tokens, stem_table, conv_weight, gain_in, gain_mid, point_weight):
    row_count = tokens.shape[1]
    kinds, width = stem_table.shape[1:]
    depth, inner = conv_weight.shape[1:]
    count, groups = lax.axis_size("dp"), lax.axis_size("groups")
    strand = lax.axis_index("strand")
    half = width // 2
    vmem = pl.BlockSpec(memory_space=pltpu.VMEM)
    anywhere = pl.BlockSpec(memory_space=pl.ANY)
    bf16, f32 = jnp.bfloat16, jnp.float32
    params = pltpu.CompilerParams(vmem_limit_bytes=24 * MIB)

    members = count * lax.axis_size("seq")
    piece_rows = point_weight.shape[0] // groups
    spread, piece = pl.pallas_call(
        send_kernel,
        out_shape=[
            jax.ShapeDtypeStruct((members, 1, row_count), tokens.dtype),
            jax.ShapeDtypeStruct((piece_rows, half), bf16),
        ],
        in_specs=[anywhere] * 2,
        out_specs=[vmem] * 2,
        scratch_shapes=[pltpu.VMEM(tokens.shape, tokens.dtype), pltpu.SemaphoreType.DMA((2,))],
        compiler_params=params,
        cost_estimate=cost("early"),
        name="send",
    )(in_hbm(tokens), in_hbm(point_weight))
    bases = lax.all_to_all(spread, ("dp", "seq"), 0, 0, tiled=True)
    table_rows = 16 * kinds
    table, plain, gain_here, weight = pl.pallas_call(
        load_kernel,
        out_shape=[
            pltpu.VMEM((table_rows, width), bf16),
            pltpu.VMEM((table_rows, half), bf16),
            pltpu.VMEM((1, depth), f32),
            pltpu.VMEM(conv_weight.shape, bf16),
        ],
        in_specs=[anywhere] * 3,
        out_specs=[vmem] * 4,
        scratch_shapes=[
            pltpu.VMEM(stem_table.shape, bf16),
            pltpu.VMEM(gain_in.shape, f32),
            pltpu.VMEM((table_rows, width), bf16),
            pltpu.SemaphoreType.DMA((2 + len(weight_parts(conv_weight)),)),
        ],
        compiler_params=params,
        cost_estimate=cost("early"),
        name="load",
    )(in_hbm(stem_table), in_hbm(gain_in), in_hbm(conv_weight))
    crossed = [lax.ppermute(piece, "dp", ring_pairs("dp", -step)) for step in range(1, count)]

    received = [[] for _ in CHUNKS]
    part = None
    for step in range(1, count):
        for index, (low, size) in enumerate(CHUNKS):
            rows = row_count // DILATION * size
            operands = [bases] + [pinned(x) for x in (table, gain_here, weight)]
            shapes = [jax.ShapeDtypeStruct((rows, inner), bf16)]
            if not index:
                operands.append(crossed[step - 1])
                shapes.append(jax.ShapeDtypeStruct(crossed[step - 1].shape, bf16))
            if part is not None:
                operands.append(part)
            part, *passed = pl.pallas_call(
                functools.partial(chunk_kernel, step, low, size, row_count, len(operands)),
                out_shape=shapes,
                in_specs=[vmem] * 4 + [anywhere] * (len(operands) - 4),
                out_specs=[vmem, anywhere][: len(shapes)],
                scratch_shapes=[pltpu.VMEM((rows + 2 * size, depth), bf16)],
                input_output_aliases={} if index else {4: 1},
                compiler_params=params,
                cost_estimate=cost(f"sent{index}"),
                name="conv_sent",
            )(*operands)
            if passed:
                crossed[step - 1] = passed[0]
            received[index].append(lax.ppermute(part, "dp", ring_pairs("dp", step)))

    places, pieces = [(0, 0)], [in_hbm(point_weight)]
    for step in range(1, count):
        for turn in range(groups):
            piece = crossed[step - 1]
            if turn:
                piece = lax.ppermute(piece, "groups", ring_pairs("groups", -turn))
            places.append((step, turn))
            pieces.append(piece)

    own, res, point = pl.pallas_call(
        functools.partial(own_kernel, places, piece_rows),
        out_shape=[
            jax.ShapeDtypeStruct((row_count, inner), f32),
            jax.ShapeDtypeStruct((row_count, half), f32),
            jax.ShapeDtypeStruct((inner, half), bf16),
        ],
        in_specs=[vmem] * 5 + [anywhere] * (1 + len(pieces)),
        out_specs=[vmem] * 3,
        scratch_shapes=[
            pltpu.VMEM((row_count + 2 * DILATION, depth), bf16),
            pltpu.SemaphoreType.DMA((len(pieces),)),
        ],
        compiler_params=params,
        cost_estimate=cost("own"),
        name="conv_own",
    )(bases, *[pinned(x) for x in (table, plain, gain_here, weight)], part, *pieces)

    out = None
    blocks = row_count // DILATION
    for index, tail in enumerate(TAILS):
        chunks = [CHUNKS[chunk] for chunk in tail]
        low, size = chunks[0][0], sum(size for _, size in chunks)
        parts = [part for chunk in tail for part in received[chunk]]
        middle = pl.pallas_call(
            functools.partial(middle_kernel, chunks, count - 1),
            out_shape=jax.ShapeDtypeStruct((blocks * size, inner), bf16),
            in_specs=[vmem] * (2 + len(parts)),
            out_specs=vmem,
            compiler_params=params,
            cost_estimate=cost(f"middle{index}"),
            name="middle",
        )(own, gain_mid, *parts)
        other = lax.ppermute(middle, "strand", ring_pairs("strand", 1))
        operands = [middle, other, res, point] + ([] if out is None else [out])
        out = pl.pallas_call(
            functools.partial(final_kernel, low, size),
            grid=(1,),
            out_shape=jax.ShapeDtypeStruct((blocks, DILATION, half), bf16),
            in_specs=[vmem] * 4 + [anywhere] * (len(operands) - 4),
            out_specs=pl.BlockSpec((blocks, size, half), lambda i, at=low // size: (0, at, 0)),
            input_output_aliases={} if out is None else {4: 0},
            compiler_params=params,
            cost_estimate=cost(f"final{index}"),
            name="final",
        )(*operands)
    return out.reshape(1, row_count, half)


def solution(mesh):
    return jax.shard_map(
        per_device,
        mesh=mesh,
        in_specs=(P(("groups", "dp"), "seq"), P(), P(None, "dp", None), P(), P(), P("dp", None)),
        out_specs=P(("groups", "dp"), "seq", "strand"),
        check_vma=False,
    )
```

profile of v0, /device:TPU:0, one launch (start us, length us, event | category | flops | bytes accessed | tf_op | source)
XLA Modules:
  0.0 40.9 jit_solution(817783389441721653)
XLA Ops:
  0.0 1.7 %send.1 = (s32[8,1,512]{2,1,0:T(1,128)}, bf16[192,768]{1,0:T(8,128)(2,1)}) custom-call(s32[1,512]{1,0:T(1,128)} %tok_any.1, bf16[384,1536]{1,0:T(8,128)(2,1)} %refs_6_.1), custom_call_target="tpu_custom_call" | custom-call | flops 100000000 | bytes 1048576 | tf_op jit(solution)/shard_map/send/pallas_call | solution.py:252
  1.7 3.0 %collective-permute-start = (bf16[192,768]{1,0:T(8,128)(2,1)}, bf16[192,768]{1,0:T(8,128)(2,1)}, u32[]{:S(2)}, u32[]{:S(2)}) collective-permute-start(bf16[192,768]{1,0:T(8,128)(2,1)} %get-tuple-element.21), channel_id=1, source_target_pairs={{0,2},{2,0},{1,3},{3,1},{4,6},{6,4},{5,7},{7,5},{8,10},{10,8},{9,1... | collective-permute-start | bytes 884744 | tf_op jit(solution)/shard_map/ppermute | solution.py:287
  4.7 4.9 %all-to-all-start = ((s32[8,1,512]{2,1,0:T(1,128)}), s32[8,1,512]{2,1,0:T(1,128)S(1)}, u32[]{:S(2)}, u32[]{:S(2)}) async-start(s32[8,1,512]{2,1,0:T(1,128)} %get-tuple-element.16), calls=%async_computation | async-start | bytes 32768 | tf_op jit(solution)/shard_map/all_to_all | solution.py:265
  9.6 2.1 %load.1 = (bf16[64,1536]{1,0:T(8,128)(2,1)S(1)}, bf16[64,768]{1,0:T(8,128)(2,1)S(1)}, f32[1,768]{1,0:T(1,128)S(1)}, bf16[3,768,768]{2,1,0:T(8,128)(2,1)S(1)}) custom-call(bf16[15,4,1536]{2,1,0:T(4,128)(2,1)} %stem_any.1, f32[1536]{0:T(1024)} %gain_any.1, bf16[3,768,768]{2,1,0:T(8,128)(2,1)} %w_any.1), custom_call_target="tpu_custom_call" | custom-call | flops 100000000 | bytes 1048576 | tf_op jit(solution)/shard_map/load/pallas_call | solution.py:267
  11.8 0.7 %copy-done = bf16[64,1536]{1,0:T(8,128)(2,1)} copy-done((bf16[64,1536]{1,0:T(8,128)(2,1)}, bf16[64,1536]{1,0:T(8,128)(2,1)S(1)}, u32[]{:S(2)}) %copy-start) | copy-done | bytes 196632
  12.4 0.6 %copy-done.2 = f32[1,768]{1,0:T(1,128)} copy-done((f32[1,768]{1,0:T(1,128)}, f32[1,768]{1,0:T(1,128)S(1)}, u32[]{:S(2)}) %copy-start.2) | copy-done | bytes 3096
  13.0 0.6 %copy-done.5 = bf16[64,768]{1,0:T(8,128)(2,1)} copy-done((bf16[64,768]{1,0:T(8,128)(2,1)}, bf16[64,768]{1,0:T(8,128)(2,1)S(1)}, u32[]{:S(2)}) %copy-start.5) | copy-done | bytes 98328
  13.6 2.6 %all-to-all-done.refs_0_ = s32[8,1,512]{2,1,0:T(1,128)S(1)} async-done(((s32[8,1,512]{2,1,0:T(1,128)}), s32[8,1,512]{2,1,0:T(1,128)S(1)}, u32[]{:S(2)}, u32[]{:S(2)}) %all-to-all-start) | async-done | bytes 16416 | tf_op jit(solution)/shard_map/all_to_all | solution.py:265
  16.2 0.9 %copy-done.1 = bf16[64,1536]{1,0:T(8,128)(2,1)S(1)} copy-done((bf16[64,1536]{1,0:T(8,128)(2,1)S(1)}, bf16[64,1536]{1,0:T(8,128)(2,1)}, u32[]{:S(2)}) %copy-start.1) | copy-done | bytes 196632
  17.1 0.7 %copy-done.3 = f32[1,768]{1,0:T(1,128)S(1)} copy-done((f32[1,768]{1,0:T(1,128)S(1)}, f32[1,768]{1,0:T(1,128)}, u32[]{:S(2)}) %copy-start.3) | copy-done | bytes 3096
  17.8 1.6 %conv_sent.3 = (bf16[128,768]{1,0:T(8,128)(2,1)S(1)}, bf16[192,768]{1,0:T(8,128)(2,1)}) custom-call(s32[8,1,512]{2,1,0:T(1,128)S(1)} %all-to-all-done.refs_0_, bf16[64,1536]{1,0:T(8,128)(2,1)S(1)} %copy-done.1, f32[1,768]{1,0:T(1,128)S(1)} %copy-done.3, bf16[3,768,768]{2,1,0:T(8,128)(2,1)S(1)} %get-tuple-element.20.refs_3_.refs_4_, ...), custom_call_target="tpu_custom_call", output_to_operand_aliasing={{1}: (4, {})} | custom-call | flops 5000000000 | bytes 1048576 | tf_op jit(solution)/shard_map/conv_sent/pallas_call | solution.py:301
  19.4 0.6 %collective-permute-start.4 = (bf16[128,768]{1,0:T(8,128)(2,1)S(1)}, bf16[128,768]{1,0:T(8,128)(2,1)S(1)}, u32[]{:S(2)}, u32[]{:S(2)}) collective-permute-start(bf16[128,768]{1,0:T(8,128)(2,1)S(1)} %get-tuple-element.22.refs_4_), channel_id=1, source_target_pairs={{0,2},{2,0},{1,3},{3,1},{4,6},{6,4},{5,7},{7,5},{8,10},{10,8},{9,1... | collective-permute-start | bytes 589832 | tf_op jit(solution)/shard_map/ppermute | solution.py:314
  20.1 1.5 %collective-permute-start.1 = (bf16[192,768]{1,0:T(8,128)(2,1)}, bf16[192,768]{1,0:T(8,128)(2,1)S(1)}, u32[]{:S(2)}, u32[]{:S(2)}) collective-permute-start(bf16[192,768]{1,0:T(8,128)(2,1)} %get-tuple-element.23.refs_7_), channel_id=1, source_target_pairs={{0,16},{16,0},{1,17},{17,1},{2,18},{18,2},{3,19},{19,3},{4,20},{20... | collective-permute-start | bytes 884744 | tf_op jit(solution)/shard_map/ppermute | solution.py:321
  21.6 2.0 %conv_sent.4.refs_4_ = bf16[256,768]{1,0:T(8,128)(2,1)S(1)} custom-call(s32[8,1,512]{2,1,0:T(1,128)S(1)} %all-to-all-done.refs_0_, bf16[64,1536]{1,0:T(8,128)(2,1)S(1)} %copy-done.1, f32[1,768]{1,0:T(1,128)S(1)} %copy-done.3, bf16[3,768,768]{2,1,0:T(8,128)(2,1)S(1)} %get-tuple-element.20.refs_3_.refs_4_, bf16[128,768]{1,0:T(8,128)(2,1)S(1)} %get-tuple-element.22.refs_4_), custom_call_target="tpu_custom_call" | custom-call | flops 15000000512 | bytes 1048576 | tf_op jit(solution)/shard_map/conv_sent/pallas_call | solution.py:301
  23.7 1.5 %collective-permute-start.5 = (bf16[256,768]{1,0:T(8,128)(2,1)S(1)}, bf16[256,768]{1,0:T(8,128)(2,1)S(1)}, u32[]{:S(2)}, u32[]{:S(2)}) collective-permute-start(bf16[256,768]{1,0:T(8,128)(2,1)S(1)} %conv_sent.4.refs_4_), channel_id=1, source_target_pairs={{0,2},{2,0},{1,3},{3,1},{4,6},{6,4},{5,7},{7,5},{8,10},{10,8},{9,1... | collective-permute-start | bytes 1179656 | tf_op jit(solution)/shard_map/ppermute | solution.py:314
  25.2 1.6 %conv_sent.5.refs_5_ = bf16[128,768]{1,0:T(8,128)(2,1)S(1)} custom-call(s32[8,1,512]{2,1,0:T(1,128)S(1)} %all-to-all-done.refs_0_, bf16[64,1536]{1,0:T(8,128)(2,1)S(1)} %copy-done.1, f32[1,768]{1,0:T(1,128)S(1)} %copy-done.3, bf16[3,768,768]{2,1,0:T(8,128)(2,1)S(1)} %get-tuple-element.20.refs_3_.refs_4_, bf16[256,768]{1,0:T(8,128)(2,1)S(1)} %conv_sent.4.refs_4_), custom_call_target="tpu_custom_call" | custom-call | flops 500000000 | bytes 1048576 | tf_op jit(solution)/shard_map/conv_sent/pallas_call | solution.py:301
  26.8 0.6 %collective-permute-start.2 = (bf16[128,768]{1,0:T(8,128)(2,1)S(1)}, bf16[128,768]{1,0:T(8,128)(2,1)S(1)}, u32[]{:S(2)}, u32[]{:S(2)}) collective-permute-start(bf16[128,768]{1,0:T(8,128)(2,1)S(1)} %conv_sent.5.refs_5_), channel_id=1, source_target_pairs={{0,2},{2,0},{1,3},{3,1},{4,6},{6,4},{5,7},{7,5},{8,10},{10,8},{9,1... | collective-permute-start | bytes 589832 | tf_op jit(solution)/shard_map/ppermute | solution.py:314
  27.4 4.1 %conv_own.1 = (f32[512,768]{1,0:T(8,128)S(1)}, f32[512,768]{1,0:T(8,128)S(1)}, bf16[768,768]{1,0:T(8,128)(2,1)S(1)}) custom-call(s32[8,1,512]{2,1,0:T(1,128)S(1)} %all-to-all-done.refs_0_, bf16[64,1536]{1,0:T(8,128)(2,1)S(1)} %copy-done.1, bf16[64,768]{1,0:T(8,128)(2,1)S(1)} %copy-done.6, f32[1,768]{1,0:T(1,128)S(1)} %copy-done.4, ...), custom_call_target="tpu_custom_call" | custom-call | flops 15000000512 | bytes 1048576 | tf_op jit(solution)/shard_map/conv_own/pallas_call | solution.py:325
  31.5 4.2 %collective-permute-done.5.refs_1_ = bf16[256,768]{1,0:T(8,128)(2,1)S(1)} collective-permute-done((bf16[256,768]{1,0:T(8,128)(2,1)S(1)}, bf16[256,768]{1,0:T(8,128)(2,1)S(1)}, u32[]{:S(2)}, u32[]{:S(2)}) %collective-permute-start.5) | collective-permute-done | bytes 393248 | tf_op jit(solution)/shard_map/ppermute | solution.py:314
  35.7 0.6 %middle.3.mine_ref = bf16[384,768]{1,0:T(8,128)(2,1)S(1)} custom-call(f32[512,768]{1,0:T(8,128)S(1)} %get-tuple-element.24.own_ref, f32[768]{0:T(1024)S(1)} %copy-done.7, bf16[128,768]{1,0:T(8,128)(2,1)S(1)} %collective-permute-done.4.refs_0_, bf16[256,768]{1,0:T(8,128)(2,1)S(1)} %collective-permute-done.5.refs_1_), custom_call_target="tpu_custom_call" | custom-call | flops 5000000000 | bytes 1048576 | tf_op jit(solution)/shard_map/middle/pallas_call | solution.py:349
  36.4 1.4 %collective-permute-done.2.refs_0_ = bf16[128,768]{1,0:T(8,128)(2,1)S(1)} collective-permute-done((bf16[128,768]{1,0:T(8,128)(2,1)S(1)}, bf16[128,768]{1,0:T(8,128)(2,1)S(1)}, u32[]{:S(2)}, u32[]{:S(2)}) %collective-permute-start.2) | collective-permute-done | bytes 196640 | tf_op jit(solution)/shard_map/ppermute | solution.py:314
  37.8 0.2 middle.2.mine_ref
  38.4 1.5 %final.2.refs_0_ = bf16[2,256,768]{2,1,0:T(8,128)(2,1)} custom-call(bf16[384,768]{1,0:T(8,128)(2,1)S(1)} %middle.3.mine_ref, bf16[384,768]{1,0:T(8,128)(2,1)S(1)} %collective-permute-done.6.other_ref, f32[512,768]{1,0:T(8,128)S(1)} %get-tuple-element.25.res_ref, bf16[768,768]{1,0:T(8,128)(2,1)S(1)} %get-tuple-element.26.point_ref), custom_call_target="tpu_custom_call" | custom-call | flops 2000000000 | bytes 1048576 | tf_op jit(solution)/shard_map/final/pallas_call | solution.py:360
  39.8 1.0 %final.3 = bf16[2,256,768]{2,1,0:T(8,128)(2,1)} custom-call(bf16[128,768]{1,0:T(8,128)(2,1)S(1)} %middle.2.mine_ref, bf16[128,768]{1,0:T(8,128)(2,1)S(1)} %collective-permute-done.3.other_ref, f32[512,768]{1,0:T(8,128)S(1)} %get-tuple-element.25.res_ref, bf16[768,768]{1,0:T(8,128)(2,1)S(1)} %get-tuple-element.26.point_ref, ...), custom_call_target="tpu_custom_call", output_to_operand_aliasing={{}: (4, {})} | custom-call | flops 5000000000 | bytes 1048576 | tf_op jit(solution)/shard_map/final/pallas_call | solution.py:360
  (18 shorter events, 0.4 us)
Async XLA Ops:
  1.7 14.5 %collective-permute-start = (bf16[192,768]{1,0:T(8,128)(2,1)}, bf16[192,768]{1,0:T(8,128)(2,1)}, u32[]{:S(2)}, u32[]{:S(2)}) collective-permute-start(bf16[192,768]{1,0:T(8,128)(2,1)} %get-tuple-element.21), channel_id=1, source_target_pairs={{0,2},{2,0},{1,3},{3,1},{4,6},{6,4},{5,7},{7,5},{8,10},{10,8},{9,1... | collective-permute-start | bytes 884744 | tf_op jit(solution)/shard_map/ppermute | solution.py:287
  4.7 11.5 %all-to-all-start = ((s32[8,1,512]{2,1,0:T(1,128)}), s32[8,1,512]{2,1,0:T(1,128)S(1)}, u32[]{:S(2)}, u32[]{:S(2)}) async-start(s32[8,1,512]{2,1,0:T(1,128)} %get-tuple-element.16), calls=%async_computation | async-start | bytes 32768 | tf_op jit(solution)/shard_map/all_to_all | solution.py:265
  11.8 0.7 %copy-start = (bf16[64,1536]{1,0:T(8,128)(2,1)}, bf16[64,1536]{1,0:T(8,128)(2,1)S(1)}, u32[]{:S(2)}) copy-start(bf16[64,1536]{1,0:T(8,128)(2,1)S(1)} %get-tuple-element.17.refs_1_) | copy-start | bytes 589828
  12.4 0.6 %copy-start.2 = (f32[1,768]{1,0:T(1,128)}, f32[1,768]{1,0:T(1,128)S(1)}, u32[]{:S(2)}) copy-start(f32[1,768]{1,0:T(1,128)S(1)} %get-tuple-element.19.refs_2_.refs_3_) | copy-start | bytes 9220
  13.0 0.6 %copy-start.5 = (bf16[64,768]{1,0:T(8,128)(2,1)}, bf16[64,768]{1,0:T(8,128)(2,1)S(1)}, u32[]{:S(2)}) copy-start(bf16[64,768]{1,0:T(8,128)(2,1)S(1)} %get-tuple-element.18.refs_2_) | copy-start | bytes 294916
  16.2 0.9 %copy-start.1 = (bf16[64,1536]{1,0:T(8,128)(2,1)S(1)}, bf16[64,1536]{1,0:T(8,128)(2,1)}, u32[]{:S(2)}) copy-start(bf16[64,1536]{1,0:T(8,128)(2,1)} %copy-done) | copy-start | bytes 589828
  17.1 0.7 %copy-start.3 = (f32[1,768]{1,0:T(1,128)S(1)}, f32[1,768]{1,0:T(1,128)}, u32[]{:S(2)}) copy-start(f32[1,768]{1,0:T(1,128)} %copy-done.2) | copy-start | bytes 9220
  19.4 12.1 %collective-permute-start.4 = (bf16[128,768]{1,0:T(8,128)(2,1)S(1)}, bf16[128,768]{1,0:T(8,128)(2,1)S(1)}, u32[]{:S(2)}, u32[]{:S(2)}) collective-permute-start(bf16[128,768]{1,0:T(8,128)(2,1)S(1)} %get-tuple-element.22.refs_4_), channel_id=1, source_target_pairs={{0,2},{2,0},{1,3},{3,1},{4,6},{6,4},{5,7},{7,5},{8,10},{10,8},{9,1... | collective-permute-start | bytes 589832 | tf_op jit(solution)/shard_map/ppermute | solution.py:314
  20.1 7.4 %collective-permute-start.1 = (bf16[192,768]{1,0:T(8,128)(2,1)}, bf16[192,768]{1,0:T(8,128)(2,1)S(1)}, u32[]{:S(2)}, u32[]{:S(2)}) collective-permute-start(bf16[192,768]{1,0:T(8,128)(2,1)} %get-tuple-element.23.refs_7_), channel_id=1, source_target_pairs={{0,16},{16,0},{1,17},{17,1},{2,18},{18,2},{3,19},{19,3},{4,20},{20... | collective-permute-start | bytes 884744 | tf_op jit(solution)/shard_map/ppermute | solution.py:321
  23.6 3.8 %copy-start.4 = (f32[1,768]{1,0:T(1,128)S(1)}, f32[1,768]{1,0:T(1,128)}, u32[]{:S(2)}) copy-start(f32[1,768]{1,0:T(1,128)} %copy-done.2) | copy-start | bytes 9220
  23.6 3.8 %copy-start.6 = (bf16[64,768]{1,0:T(8,128)(2,1)S(1)}, bf16[64,768]{1,0:T(8,128)(2,1)}, u32[]{:S(2)}) copy-start(bf16[64,768]{1,0:T(8,128)(2,1)} %copy-done.5) | copy-start | bytes 294916
  23.7 12.0 %collective-permute-start.5 = (bf16[256,768]{1,0:T(8,128)(2,1)S(1)}, bf16[256,768]{1,0:T(8,128)(2,1)S(1)}, u32[]{:S(2)}, u32[]{:S(2)}) collective-permute-start(bf16[256,768]{1,0:T(8,128)(2,1)S(1)} %conv_sent.4.refs_4_), channel_id=1, source_target_pairs={{0,2},{2,0},{1,3},{3,1},{4,6},{6,4},{5,7},{7,5},{8,10},{10,8},{9,1... | collective-permute-start | bytes 1179656 | tf_op jit(solution)/shard_map/ppermute | solution.py:314
  26.8 11.0 %collective-permute-start.2 = (bf16[128,768]{1,0:T(8,128)(2,1)S(1)}, bf16[128,768]{1,0:T(8,128)(2,1)S(1)}, u32[]{:S(2)}, u32[]{:S(2)}) collective-permute-start(bf16[128,768]{1,0:T(8,128)(2,1)S(1)} %conv_sent.5.refs_5_), channel_id=1, source_target_pairs={{0,2},{2,0},{1,3},{3,1},{4,6},{6,4},{5,7},{7,5},{8,10},{10,8},{9,1... | collective-permute-start | bytes 589832 | tf_op jit(solution)/shard_map/ppermute | solution.py:314
  27.4 8.3 %copy-start.7 = (f32[768]{0:T(1024)S(1)}, f32[768]{0:T(1024)}, u32[]{:S(2)}) copy-start(f32[768]{0:T(1024)} %gain_ref.3) | copy-start | bytes 9220
  36.3 2.1 %collective-permute-start.6 = (bf16[384,768]{1,0:T(8,128)(2,1)S(1)}, bf16[384,768]{1,0:T(8,128)(2,1)S(1)}, u32[]{:S(2)}, u32[]{:S(2)}) collective-permute-start(bf16[384,768]{1,0:T(8,128)(2,1)S(1)} %middle.3.mine_ref), channel_id=1, source_target_pairs={{0,1},{1,0},{2,3},{3,2},{4,5},{5,4},{6,7},{7,6},{8,9},{9,8},{10,11... | collective-permute-start | bytes 1769480 | tf_op jit(solution)/shard_map/ppermute | solution.py:358
  38.1 1.8 %collective-permute-start.3 = (bf16[128,768]{1,0:T(8,128)(2,1)S(1)}, bf16[128,768]{1,0:T(8,128)(2,1)S(1)}, u32[]{:S(2)}, u32[]{:S(2)}) collective-permute-start(bf16[128,768]{1,0:T(8,128)(2,1)S(1)} %middle.2.mine_ref), channel_id=1, source_target_pairs={{0,1},{1,0},{2,3},{3,2},{4,5},{5,4},{6,7},{7,6},{8,9},{9,8},{10,11... | collective-permute-start | bytes 589832 | tf_op jit(solution)/shard_map/ppermute | solution.py:358
where the time goes:
time: 41.1 us; the launch traced here: 40.9 us
  Pallas kernels  16.5 us (40%)
  starting transfers between devices  12.3 us (30%)
  waiting for transfers between devices  8.42 us (20%)
  local copies, waits for them, and re-layouts  3.49 us (8%)
    ppermute x3, waiting for transfers between devices, per_device(): received[index].append(lax.ppermute(part, 'dp', ring_pairs('dp', step)))  5.61 us
    pallas_call x3, Pallas kernels, per_device(): pl.pallas_call(functools.partial(chunk_kernel, step, low, size, row_count...  5.28 us
    all_to_all x1, starting transfers between devices, per_device(): bases = lax.all_to_all(spread, ('dp', 'seq'), 0, 0, tiled=True)  4.88 us
    pallas_call x1, Pallas kernels, per_device(): pl.pallas_call(functools.partial(own_kernel, places, piece_rows), out_sha...  4.05 us
    unnamed x16, local copies, waits for them, and re-layouts  3.49 us
    ppermute x1, starting transfers between devices, per_device(): lax.ppermute(piece, 'dp', ring_pairs('dp', -step))  3 us
    ppermute x3, starting transfers between devices, per_device(): received[index].append(lax.ppermute(part, 'dp', ring_pairs('dp', step)))  2.78 us
    all_to_all x1, waiting for transfers between devices, per_device(): bases = lax.all_to_all(spread, ('dp', 'seq'), 0, 0, tiled=True)  2.56 us
  transfers between devices with their start and end apart: 8, of which 4 were waited for; matrix products, arithmetic and copies ran while one was open for 0% of the time, Pallas kernels for 30%

commit v1 on v0

--- a/solution.py
+++ b/solution.py
@@ -10,21 +10,28 @@
 DILATION = 256
 EPS = 1e-06
 ROW_STEP = 128
-CHUNKS = ((0, 64), (64, 128), (192, 64))
+CHUNKS = ((0, 96), (96, 96), (192, 64))
 TAILS = ((0, 1), (2,))
 KINDS = 4
+TABLE = 16 * KINDS
 FLOPS = {
     "early": 0.1,
-    "sent0": 5.0,
-    "sent1": 15.0,
-    "sent2": 0.5,
+    "load": 0.1,
+    "sent0": 15.0,
+    "sent1": 0.5,
+    "sent2": 15.0,
     "own": 15.0,
-    "middle0": 5.0,
+    "middle0": 0.05,
     "middle1": 5.0,
-    "final0": 2.0,
-    "final1": 5.0,
+    "final0": 0.5,
+    "final1": 15.0,
 }
 MIB = 2**20
+
+
+def line_pairs(axis, distance):
+    count = lax.axis_size(axis)
+    return [(i, i + distance) for i in range(count) if 0 <= i + distance < count]
 
 
 def ring_pairs(axis, distance):
@@ -32,12 +39,10 @@
     return [(i, (i + distance) % count) for i in range(count)]
 
 
-def base_taps(tok_ref, step, row_count):
-    count, blocks = lax.axis_size("dp"), lax.axis_size("seq")
-    here = lax.axis_index("seq")
-    first = lax.rem(lax.axis_index("dp") + step, count) * blocks
-    sides = [jnp.maximum(here - 1, 0), here, jnp.minimum(here + 1, blocks - 1)]
-    bases = jnp.concatenate([tok_ref[first + side] for side in sides], axis=1)
+def base_taps(sides, step, row_count):
+    blocks, here = lax.axis_size("seq"), lax.axis_index("seq")
+    low = step * row_count
+    bases = jnp.concatenate([ref[:, low : low + row_count] for ref in sides], axis=1)
     width, span = 3 * row_count, row_count + 2 * DILATION
     spread = jnp.broadcast_to(bases, (16, width))
     start = width - (row_count - DILATION + 8)
@@ -49,9 +54,9 @@
     return jnp.where(inside, taps, -1).astype(jnp.float32).astype(jnp.bfloat16)
 
 
-def one_hot(taps, second, table_rows):
-    row = lax.broadcasted_iota(jnp.int32, (table_rows, 16), 0) // KINDS
-    column = lax.broadcasted_iota(jnp.int32, (table_rows, 16), 1)
+def one_hot(taps, second):
+    row = lax.broadcasted_iota(jnp.int32, (TABLE, 16), 0) // KINDS
+    column = lax.broadcasted_iota(jnp.int32, (TABLE, 16), 1)
     chosen = (column == 15 - row + second * (2 * row - 14)).astype(jnp.float32)
     values = jnp.dot(chosen.astype(jnp.bfloat16), taps, preferred_element_type=jnp.float32)
     base = lax.broadcasted_iota(jnp.int32, values.shape, 0) % KINDS
@@ -65,53 +70,69 @@
     return half + half * jnp.tanh(inner)
 
 
-def activate(hot, table_ref, gain_ref, act_ref):
-    depth = gain_ref.shape[1]
+def activate(hot, gain_ref, pack_ref, act_ref):
+    depth, width = act_ref.shape[1], gain_ref.shape[0]
+    turn = lax.rem(width - lax.axis_index("dp") * depth, width)
+    gain = jnp.broadcast_to(gain_ref[...].reshape(1, width), (8, width))
+    gain = pltpu.roll(gain, turn, 1)[:1, :depth]
+    tables = [pack_ref[rows] for rows in table_rows(depth, width, pack_ref.shape[1])]
     for start in range(0, hot.shape[0], ROW_STEP):
-        embedded = jnp.dot(
-            hot[start : start + ROW_STEP], table_ref[...], preferred_element_type=jnp.float32
-        )
-        mean = jnp.mean(embedded * embedded, axis=-1, keepdims=True)
-        scaled = embedded[:, :depth] * lax.rsqrt(mean + EPS) * gain_ref[...]
+        rows = hot[start : start + ROW_STEP]
+        parts = [jnp.dot(rows, table, preferred_element_type=jnp.float32) for table in tables]
+        mean = sum(jnp.sum(part * part, axis=-1, keepdims=True) for part in parts) * (1.0 / width)
+        scaled = parts[0][:, :depth] * lax.rsqrt(mean + EPS) * gain
         act_ref[start : start + ROW_STEP] = gelu(scaled).astype(jnp.bfloat16)
 
 
-def convolve(blocks, w_ref):
+def convolve(blocks, pack_ref):
     second = lax.axis_index("strand")
     total = None
     for tap, block in enumerate(blocks):
-        weight = w_ref[tap + second * (2 - 2 * tap)]
+        depth = block.shape[1]
+        row = pl.multiple_of((tap + second * (2 - 2 * tap)) * depth, 16)
+        weight = pack_ref[pl.ds(row, depth), :]
         part = jnp.dot(block, weight, preferred_element_type=jnp.float32)
         total = part if total is None else total + part
     return total
 
 
-def send_kernel(tok_any, point_any, spread_ref, piece_ref, tok_ref, sems):
+def table_rows(depth, width, columns):
+    first = 3 * depth
+    count = width // columns
+    return [slice(first + i * TABLE, first + (i + 1) * TABLE) for i in range(count)]
+
+
+def plain_rows(depth, width, columns):
+    first = 3 * depth + width // columns * TABLE
+    return slice(first, first + TABLE)
+
+
+def slice_kernel(point_any, tok_any, piece_ref, tok_ref, sems):
     rows, columns = piece_ref.shape
     low = pl.multiple_of(lax.axis_index("groups") * rows, 16)
     left = pl.multiple_of(lax.axis_index("strand") * columns, 128)
     part = point_any.at[pl.ds(low, rows), pl.ds(left, columns)]
     copies = [
-        pltpu.make_async_copy(tok_any, tok_ref, sems.at[0]),
-        pltpu.make_async_copy(part, piece_ref, sems.at[1]),
+        pltpu.make_async_copy(part, piece_ref, sems.at[0]),
+        pltpu.make_async_copy(tok_any, tok_ref, sems.at[1]),
     ]
     for copy in copies:
         copy.start()
-    copies[0].wait()
-    spread_ref[...] = jnp.broadcast_to(tok_ref[...][None], spread_ref.shape)
-    copies[1].wait()
-
-
-def load_kernel(stem_any, gain_any, w_any, table_ref, plain_ref, gain_here_ref, w_ref, *scratch):
-    stem_ref, gain_ref, flat_ref, sems = scratch
-    depth = w_any.shape[1]
-    copies = [
-        pltpu.make_async_copy(stem_any, stem_ref, sems.at[0]),
-        pltpu.make_async_copy(gain_any, gain_ref, sems.at[1]),
-    ]
+    for copy in copies:
+        copy.wait()
+
+
+def join_kernel(*refs):
+    refs[-1][...] = jnp.concatenate([ref[...] for ref in refs[:-1]], axis=1)
+
+
+def load_kernel(stem_any, w_any, pack_ref, stem_ref, flat_ref, sems):
+    depth, columns = w_any.shape[1:]
+    copies = [pltpu.make_async_copy(stem_any, stem_ref, sems.at[0])]
     for index, (tap, low, rows) in enumerate(weight_parts(w_any)):
-        part = (tap, pl.ds(low, rows))
-        copies.append(pltpu.make_async_copy(w_any.at[part], w_ref.at[part], sems.at[index + 2]))
+        source = w_any.at[tap, pl.ds(low, rows)]
+        target = pack_ref.at[pl.ds(tap * depth + low, rows)]
+        copies.append(pltpu.make_async_copy(source, target, sems.at[index + 1]))
     for copy in copies:
         copy.start()
     copies[0].wait()
@@ -120,16 +141,13 @@
     slabs += [jnp.zeros((kinds, width), jnp.float32)] * (16 - taps)
     flat = jnp.concatenate(slabs)
     flat_ref[...] = flat.astype(jnp.bfloat16)
-    left = lax.axis_index("dp") * depth
-    turn = lax.rem(width - left, width)
-    table_ref[...] = pltpu.roll(flat, turn, 1).astype(jnp.bfloat16)
-    copies[1].wait()
-    gain = jnp.broadcast_to(gain_ref[...].reshape(1, width), (8, width))
-    gain_here_ref[...] = pltpu.roll(gain, turn, 1)[:1, :depth]
-    half = plain_ref.shape[1]
-    column = pl.multiple_of(lax.axis_index("strand") * half, 128)
-    plain_ref[...] = flat_ref[:, pl.ds(column, half)]
-    for copy in copies[2:]:
+    turn = lax.rem(width - lax.axis_index("dp") * depth, width)
+    turned = pltpu.roll(flat, turn, 1).astype(jnp.bfloat16)
+    for index, rows in enumerate(table_rows(depth, width, columns)):
+        pack_ref[rows] = turned[:, index * columns : (index + 1) * columns]
+    column = pl.multiple_of(lax.axis_index("strand") * columns, 128)
+    pack_ref[plain_rows(depth, width, columns)] = flat_ref[:, pl.ds(column, columns)]
+    for copy in copies[1:]:
         copy.wait()
 
 
@@ -139,15 +157,14 @@
 
 
 def chunk_kernel(step, low, size, row_count, out_index, *refs):
-    tok_ref, table_ref, gain_ref, w_ref = refs[:4]
+    gain_ref, pack_ref = refs[3:5]
     out_ref, act_ref = refs[out_index], refs[-1]
-    taps = base_taps(tok_ref, step, row_count)
-    hot = one_hot(taps, lax.axis_index("strand"), table_ref.shape[0])
+    hot = one_hot(base_taps(refs[:3], step, row_count), lax.axis_index("strand"))
     blocks = row_count // DILATION
     pieces = [hot[b * DILATION + low :][:size] for b in range(blocks + 2)]
-    activate(jnp.concatenate(pieces).astype(jnp.bfloat16), table_ref, gain_ref, act_ref)
+    activate(jnp.concatenate(pieces).astype(jnp.bfloat16), gain_ref, pack_ref, act_ref)
     parts = [act_ref[t * size : (t + blocks) * size] for t in range(3)]
-    out_ref[...] = convolve(parts, w_ref).astype(jnp.bfloat16)
+    out_ref[...] = convolve(parts, pack_ref).astype(jnp.bfloat16)
 
 
 def rows_of(ref, low, size):
@@ -166,7 +183,7 @@
 
 
 def own_kernel(places, piece_rows, *refs):
-    tok_ref, table_ref, plain_ref, gain_ref, w_ref = refs[:5]
+    gain_ref, pack_ref = refs[3:5]
     pieces = refs[6 : 6 + len(places)]
     out_ref, res_ref, point_ref, act_ref, sems = refs[6 + len(places) :]
     ranks, groups = lax.axis_size("dp"), lax.axis_size("groups")
@@ -186,16 +203,15 @@
         copies[-1].start()
     row_count = out_ref.shape[0]
     second = lax.axis_index("strand")
-    taps = base_taps(tok_ref, 0, row_count)
-    hot = one_hot(taps, second, table_ref.shape[0])
+    taps = base_taps(refs[:3], 0, row_count)
+    hot = one_hot(taps, second)
     here = slice(DILATION, DILATION + row_count)
-    both = hot[here] + one_hot(taps[:, here], 1 - second, table_ref.shape[0])
-    res_ref[...] = jnp.dot(
-        both.astype(jnp.bfloat16), plain_ref[...], preferred_element_type=jnp.float32
-    )
-    activate(hot.astype(jnp.bfloat16), table_ref, gain_ref, act_ref)
+    both = (hot[here] + one_hot(taps[:, here], 1 - second)).astype(jnp.bfloat16)
+    plain = pack_ref[plain_rows(act_ref.shape[1], gain_ref.shape[0], pack_ref.shape[1])]
+    res_ref[...] = jnp.dot(both, plain, preferred_element_type=jnp.float32)
+    activate(hot.astype(jnp.bfloat16), gain_ref, pack_ref, act_ref)
     blocks = [act_ref[t * DILATION : t * DILATION + row_count] for t in range(3)]
-    out_ref[...] = convolve(blocks, w_ref)
+    out_ref[...] = convolve(blocks, pack_ref)
     for copy in copies:
         copy.wait()
 
@@ -221,10 +237,6 @@
     out_ref[...] = value.reshape(out_ref.shape)
 
 
-def pinned(x):
-    return pltpu.with_memory_space_constraint(x, pltpu.VMEM)
-
-
 def in_hbm(x):
     return pltpu.with_memory_space_constraint(x, pltpu.HBM)
 
@@ -237,74 +249,77 @@
 
 def per_device(tokens, stem_table, conv_weight, gain_in, gain_mid, point_weight):
     row_count = tokens.shape[1]
-    kinds, width = stem_table.shape[1:]
+    width = stem_table.shape[2]
     depth, inner = conv_weight.shape[1:]
     count, groups = lax.axis_size("dp"), lax.axis_size("groups")
-    strand = lax.axis_index("strand")
     half = width // 2
     vmem = pl.BlockSpec(memory_space=pltpu.VMEM)
     anywhere = pl.BlockSpec(memory_space=pl.ANY)
     bf16, f32 = jnp.bfloat16, jnp.float32
     params = pltpu.CompilerParams(vmem_limit_bytes=24 * MIB)
 
-    members = count * lax.axis_size("seq")
+    others = [lax.ppermute(tokens, "dp", ring_pairs("dp", -step)) for step in range(1, count)]
     piece_rows = point_weight.shape[0] // groups
-    spread, piece = pl.pallas_call(
-        send_kernel,
+    piece, here = pl.pallas_call(
+        slice_kernel,
         out_shape=[
-            jax.ShapeDtypeStruct((members, 1, row_count), tokens.dtype),
             jax.ShapeDtypeStruct((piece_rows, half), bf16),
+            jax.ShapeDtypeStruct(tokens.shape, tokens.dtype),
         ],
         in_specs=[anywhere] * 2,
         out_specs=[vmem] * 2,
-        scratch_shapes=[pltpu.VMEM(tokens.shape, tokens.dtype), pltpu.SemaphoreType.DMA((2,))],
+        scratch_shapes=[pltpu.SemaphoreType.DMA((2,))],
         compiler_params=params,
         cost_estimate=cost("early"),
-        name="send",
-    )(in_hbm(tokens), in_hbm(point_weight))
-    bases = lax.all_to_all(spread, ("dp", "seq"), 0, 0, tiled=True)
-    table_rows = 16 * kinds
-    table, plain, gain_here, weight = pl.pallas_call(
+        name="point_slice",
+    )(in_hbm(point_weight), in_hbm(tokens))
+    joined = pl.pallas_call(
+        join_kernel,
+        out_shape=jax.ShapeDtypeStruct((1, count * row_count), tokens.dtype),
+        in_specs=[vmem] * count,
+        out_specs=vmem,
+        compiler_params=params,
+        cost_estimate=cost("early"),
+        name="join",
+    )(here, *others)
+    below = lax.ppermute(joined, "seq", line_pairs("seq", 1))
+    above = lax.ppermute(joined, "seq", line_pairs("seq", -1))
+    pack_rows = 3 * depth + (width // inner + 1) * TABLE
+    pack = pl.pallas_call(
         load_kernel,
-        out_shape=[
-            pltpu.VMEM((table_rows, width), bf16),
-            pltpu.VMEM((table_rows, half), bf16),
-            pltpu.VMEM((1, depth), f32),
-            pltpu.VMEM(conv_weight.shape, bf16),
-        ],
-        in_specs=[anywhere] * 3,
-        out_specs=[vmem] * 4,
+        out_shape=jax.ShapeDtypeStruct((pack_rows, inner), bf16),
+        in_specs=[anywhere] * 2,
+        out_specs=vmem,
         scratch_shapes=[
             pltpu.VMEM(stem_table.shape, bf16),
-            pltpu.VMEM(gain_in.shape, f32),
-            pltpu.VMEM((table_rows, width), bf16),
-            pltpu.SemaphoreType.DMA((2 + len(weight_parts(conv_weight)),)),
+            pltpu.VMEM((TABLE, width), bf16),
+            pltpu.SemaphoreType.DMA((1 + len(weight_parts(conv_weight)),)),
         ],
         compiler_params=params,
-        cost_estimate=cost("early"),
+        cost_estimate=cost("load"),
         name="load",
-    )(in_hbm(stem_table), in_hbm(gain_in), in_hbm(conv_weight))
+    )(in_hbm(stem_table), in_hbm(conv_weight))
+    shared = [below, joined, above, gain_in, pack]
     crossed = [lax.ppermute(piece, "dp", ring_pairs("dp", -step)) for step in range(1, count)]
 
     received = [[] for _ in CHUNKS]
-    part = None
     for step in range(1, count):
         for index, (low, size) in enumerate(CHUNKS):
             rows = row_count // DILATION * size
-            operands = [bases] + [pinned(x) for x in (table, gain_here, weight)]
+            operands = list(shared)
             shapes = [jax.ShapeDtypeStruct((rows, inner), bf16)]
-            if not index:
+            if index == 1:
                 operands.append(crossed[step - 1])
                 shapes.append(jax.ShapeDtypeStruct(crossed[step - 1].shape, bf16))
-            if part is not None:
+            if index:
                 operands.append(part)
             part, *passed = pl.pallas_call(
                 functools.partial(chunk_kernel, step, low, size, row_count, len(operands)),
                 out_shape=shapes,
-                in_specs=[vmem] * 4 + [anywhere] * (len(operands) - 4),
+                in_specs=[vmem] * 5 + [anywhere] * (len(operands) - 5),
                 out_specs=[vmem, anywhere][: len(shapes)],
                 scratch_shapes=[pltpu.VMEM((rows + 2 * size, depth), bf16)],
-                input_output_aliases={} if index else {4: 1},
+                input_output_aliases={5: 1} if index == 1 else {},
                 compiler_params=params,
                 cost_estimate=cost(f"sent{index}"),
                 name="conv_sent",
@@ -338,7 +353,7 @@
         compiler_params=params,
         cost_estimate=cost("own"),
         name="conv_own",
-    )(bases, *[pinned(x) for x in (table, plain, gain_here, weight)], part, *pieces)
+    )(*shared, part, *pieces)
 
     out = None
     blocks = row_count // DILATION

time: 41.1 us -> 36.6 us (0.89)
  local copies, waits for them, and re-layouts: 3.49 us -> 0.01 us
  waiting for transfers between devices: 8.42 us -> 6.84 us
  starting transfers between devices: 12.3 us -> 13.7 us
  Pallas kernels: 16.5 us -> 15.7 us
    ppermute x0 -> x3, starting transfers between devices: none -> 8.24 us  [the longest x1 4.01 us: per_device(): below = lax.ppermute(joined, 'seq', line_pairs('seq', 1))]
    all_to_all x1 -> x0, starting transfers between devices: 4.88 us -> none  [per_device(): bases = lax.all_to_all(spread, ('dp', 'seq'), 0, 0, tiled=True)]
    unnamed x16 -> x4, local copies, waits for them, and re-layouts: 3.49 us -> 0.01 us
    ppermute x3, waiting for transfers between devices: 5.61 us -> 2.38 us  [per_device(): received[index].append(lax.ppermute(part, 'dp', ring_pairs('dp', step)))]
    ppermute x1, starting transfers between devices: 3 us -> 0.07 us  [per_device(): lax.ppermute(piece, 'dp', ring_pairs('dp', -step))]
    ppermute x0 -> x3, waiting for transfers between devices: none -> 2.77 us  [the longest x1 2.06 us: per_device(): above = lax.ppermute(joined, 'seq', line_pairs('seq', -1))]
    all_to_all x1 -> x0, waiting for transfers between devices: 2.56 us -> none  [per_device(): bases = lax.all_to_all(spread, ('dp', 'seq'), 0, 0, tiled=True)]
    ppermute x1, waiting for transfers between devices: 0.01 us -> 1.45 us  [per_device(): piece = lax.ppermute(piece, 'groups', ring_pairs('groups', -turn))]
  transfers between devices with their start and end apart: 8 -> 10, of which waited for: 4 -> 6; matrix products, arithmetic and copies ran while one was open for 0% -> 0% of each run, Pallas kernels for 30% -> 40%
where the time goes in v1:
time: 36.6 us; the launch traced here: 36.4 us
  Pallas kernels  15.7 us (43%)
  starting transfers between devices  13.7 us (37%)
  waiting for transfers between devices  6.84 us (19%)
    pallas_call x3, Pallas kernels, per_device(): pl.pallas_call(functools.partial(chunk_kernel, step, low, size, row_count...  5.1 us
    pallas_call x1, Pallas kernels, per_device(): pl.pallas_call(functools.partial(own_kernel, places, piece_rows), out_sha...  4.15 us
    ppermute x1, starting transfers between devices, per_device(): below = lax.ppermute(joined, 'seq', line_pairs('seq', 1))  4.01 us
    ppermute x3, starting transfers between devices, per_device(): received[index].append(lax.ppermute(part, 'dp', ring_pairs('dp', step)))  3.66 us
    ppermute x1, starting transfers between devices, per_device(): lax.ppermute(tokens, 'dp', ring_pairs('dp', -step))  2.94 us
    pallas_call x2, Pallas kernels, per_device(): pl.pallas_call(functools.partial(final_kernel, low, size), grid=(1,), out...  2.49 us
    ppermute x3, waiting for transfers between devices, per_device(): received[index].append(lax.ppermute(part, 'dp', ring_pairs('dp', step)))  2.38 us
    pallas_call x1, Pallas kernels, per_device(): pl.pallas_call(load_kernel, out_shape=jax.ShapeDtypeStruct((pack_rows, in...  2.12 us
  transfers between devices with their start and end apart: 10, of which 6 were waited for; matrix products, arithmetic and copies ran while one was open for 0% of the time, Pallas kernels for 40%

profile of v1, /device:TPU:0, one launch (start us, length us, event | category | flops | bytes accessed | tf_op | source)
XLA Modules:
  0.0 36.4 jit_solution(13741667048594319987)
XLA Ops:
  0.0 2.9 %collective-permute-start = (s32[1,512]{1,0:T(1,128)}, s32[1,512]{1,0:T(1,128)S(1)}, u32[]{:S(2)}, u32[]{:S(2)}) collective-permute-start(s32[1,512]{1,0:T(1,128)} %tok_any.1), channel_id=1, source_target_pairs={{0,2},{2,0},{1,3},{3,1},{4,6},{6,4},{5,7},{7,5},{8,10},{10,8},{9,1... | collective-permute-start | bytes 6152 | tf_op jit(solution)/shard_map/ppermute | solution.py:261
  2.9 1.0 %point_slice.1 = (bf16[192,768]{1,0:T(8,128)(2,1)S(1)}, s32[1,512]{1,0:T(1,128)S(1)}) custom-call(bf16[384,1536]{1,0:T(8,128)(2,1)} %refs_6_.1, s32[1,512]{1,0:T(1,128)} %tok_any.1), custom_call_target="tpu_custom_call" | custom-call | flops 100000000 | bytes 1048576 | tf_op jit(solution)/shard_map/point_slice/pallas_call | solution.py:263
  3.9 0.1 collective-permute-start.3
  4.0 0.7 %collective-permute-done.refs_1_ = s32[1,512]{1,0:T(1,128)S(1)} collective-permute-done((s32[1,512]{1,0:T(1,128)}, s32[1,512]{1,0:T(1,128)S(1)}, u32[]{:S(2)}, u32[]{:S(2)}) %collective-permute-start) | collective-permute-done | bytes 2080 | tf_op jit(solution)/shard_map/ppermute | solution.py:261
  4.7 4.0 %collective-permute-start.1 = (s32[1,1024]{1,0:T(1,128)S(1)}, s32[1,1024]{1,0:T(1,128)S(1)}, u32[]{:S(2)}, u32[]{:S(2)}) collective-permute-start(s32[1,1024]{1,0:T(1,128)S(1)} %join.1.refs_1_), channel_id=1, source_target_pairs={{0,4},{4,8},{8,12},{1,5},{5,9},{9,13},{2,6},{6,10},{10,14},{3,7},{... | collective-permute-start | bytes 12296 | tf_op jit(solution)/shard_map/ppermute | solution.py:285
  8.7 1.3 %collective-permute-start.2 = (s32[1,1024]{1,0:T(1,128)S(1)}, s32[1,1024]{1,0:T(1,128)S(1)}, u32[]{:S(2)}, u32[]{:S(2)}) collective-permute-start(s32[1,1024]{1,0:T(1,128)S(1)} %join.1.refs_1_), channel_id=1, source_target_pairs={{4,0},{8,4},{12,8},{5,1},{9,5},{13,9},{6,2},{10,6},{14,10},{7,3},{... | collective-permute-start | bytes 12296 | tf_op jit(solution)/shard_map/ppermute | solution.py:286
  10.0 2.1 %load.1.refs_4_ = bf16[2496,768]{1,0:T(8,128)(2,1)S(1)} custom-call(bf16[15,4,1536]{2,1,0:T(4,128)(2,1)} %stem_any.1, bf16[3,768,768]{2,1,0:T(8,128)(2,1)} %w_any.1), custom_call_target="tpu_custom_call" | custom-call | flops 100000000 | bytes 1048576 | tf_op jit(solution)/shard_map/load/pallas_call | solution.py:288
  12.2 2.1 %collective-permute-done.2.refs_2_ = s32[1,1024]{1,0:T(1,128)S(1)} collective-permute-done((s32[1,1024]{1,0:T(1,128)S(1)}, s32[1,1024]{1,0:T(1,128)S(1)}, u32[]{:S(2)}, u32[]{:S(2)}) %collective-permute-start.2) | collective-permute-done | bytes 4128 | tf_op jit(solution)/shard_map/ppermute | solution.py:286
  14.3 1.7 %conv_sent.3.refs_6_ = bf16[192,768]{1,0:T(8,128)(2,1)S(1)} custom-call(s32[1,1024]{1,0:T(1,128)S(1)} %collective-permute-done.1.refs_0_, s32[1,1024]{1,0:T(1,128)S(1)} %join.1.refs_1_, s32[1,1024]{1,0:T(1,128)S(1)} %collective-permute-done.2.refs_2_, f32[1536]{0:T(1024)S(1)} %copy-done, bf16[2496,768]{1,0:T(8,128)(2,1)S(1)} %load.1.refs_4_), custom_call_target="tpu_custom_call" | custom-call | flops 15000000512 | bytes 1048576 | tf_op jit(solution)/shard_map/conv_sent/pallas_call | solution.py:316
  16.0 1.6 %collective-permute-start.7 = (bf16[192,768]{1,0:T(8,128)(2,1)S(1)}, bf16[192,768]{1,0:T(8,128)(2,1)S(1)}, u32[]{:S(2)}, u32[]{:S(2)}) collective-permute-start(bf16[192,768]{1,0:T(8,128)(2,1)S(1)} %conv_sent.3.refs_6_), channel_id=1, source_target_pairs={{0,2},{2,0},{1,3},{3,1},{4,6},{6,4},{5,7},{7,5},{8,10},{10,8},{9,1... | collective-permute-start | bytes 884744 | tf_op jit(solution)/shard_map/ppermute | solution.py:329
  17.6 1.7 %conv_sent.4 = (bf16[192,768]{1,0:T(8,128)(2,1)S(1)}, bf16[192,768]{1,0:T(8,128)(2,1)S(1)}) custom-call(s32[1,1024]{1,0:T(1,128)S(1)} %collective-permute-done.1.refs_0_, s32[1,1024]{1,0:T(1,128)S(1)} %join.1.refs_1_, s32[1,1024]{1,0:T(1,128)S(1)} %collective-permute-done.2.refs_2_, f32[1536]{0:T(1024)S(1)} %copy-done, ...), custom_call_target="tpu_custom_call", output_to_operand_aliasing={{1}: (5, {})} | custom-call | flops 500000000 | bytes 1048576 | tf_op jit(solution)/shard_map/conv_sent/pallas_call | solution.py:316
  19.3 1.6 %collective-permute-start.4 = (bf16[192,768]{1,0:T(8,128)(2,1)S(1)}, bf16[192,768]{1,0:T(8,128)(2,1)S(1)}, u32[]{:S(2)}, u32[]{:S(2)}) collective-permute-start(bf16[192,768]{1,0:T(8,128)(2,1)S(1)} %get-tuple-element.15.refs_7_), channel_id=1, source_target_pairs={{0,16},{16,0},{1,17},{17,1},{2,18},{18,2},{3,19},{19,3},{4,20},{20... | collective-permute-start | bytes 884744 | tf_op jit(solution)/shard_map/ppermute | solution.py:336
  20.9 0.5 %collective-permute-start.8 = (bf16[192,768]{1,0:T(8,128)(2,1)S(1)}, bf16[192,768]{1,0:T(8,128)(2,1)S(1)}, u32[]{:S(2)}, u32[]{:S(2)}) collective-permute-start(bf16[192,768]{1,0:T(8,128)(2,1)S(1)} %get-tuple-element.14.refs_5_), channel_id=1, source_target_pairs={{0,2},{2,0},{1,3},{3,1},{4,6},{6,4},{5,7},{7,5},{8,10},{10,8},{9,1... | collective-permute-start | bytes 884744 | tf_op jit(solution)/shard_map/ppermute | solution.py:329
  21.4 1.6 %conv_sent.5.refs_5_ = bf16[128,768]{1,0:T(8,128)(2,1)S(1)} custom-call(s32[1,1024]{1,0:T(1,128)S(1)} %collective-permute-done.1.refs_0_, s32[1,1024]{1,0:T(1,128)S(1)} %join.1.refs_1_, s32[1,1024]{1,0:T(1,128)S(1)} %collective-permute-done.2.refs_2_, f32[1536]{0:T(1024)S(1)} %copy-done, bf16[2496,768]{1,0:T(8,128)(2,1)S(1)} %load.1.refs_4_, ...), custom_call_target="tpu_custom_call" | custom-call | flops 15000000512 | bytes 1048576 | tf_op jit(solution)/shard_map/conv_sent/pallas_call | solution.py:316
  23.1 1.6 %collective-permute-start.5 = (bf16[128,768]{1,0:T(8,128)(2,1)S(1)}, bf16[128,768]{1,0:T(8,128)(2,1)S(1)}, u32[]{:S(2)}, u32[]{:S(2)}) collective-permute-start(bf16[128,768]{1,0:T(8,128)(2,1)S(1)} %conv_sent.5.refs_5_), channel_id=1, source_target_pairs={{0,2},{2,0},{1,3},{3,1},{4,6},{6,4},{5,7},{7,5},{8,10},{10,8},{9,1... | collective-permute-start | bytes 589832 | tf_op jit(solution)/shard_map/ppermute | solution.py:329
  24.6 1.4 %collective-permute-done.4.refs_8_ = bf16[192,768]{1,0:T(8,128)(2,1)S(1)} collective-permute-done((bf16[192,768]{1,0:T(8,128)(2,1)S(1)}, bf16[192,768]{1,0:T(8,128)(2,1)S(1)}, u32[]{:S(2)}, u32[]{:S(2)}) %collective-permute-start.4) | collective-permute-done | bytes 294944 | tf_op jit(solution)/shard_map/ppermute | solution.py:336
  26.1 4.1 %conv_own.1 = (f32[512,768]{1,0:T(8,128)S(1)}, f32[512,768]{1,0:T(8,128)S(1)}, bf16[768,768]{1,0:T(8,128)(2,1)S(1)}) custom-call(s32[1,1024]{1,0:T(1,128)S(1)} %collective-permute-done.1.refs_0_, s32[1,1024]{1,0:T(1,128)S(1)} %join.1.refs_1_, s32[1,1024]{1,0:T(1,128)S(1)} %collective-permute-done.2.refs_2_, f32[1536]{0:T(1024)S(1)} %copy-done, ...), custom_call_target="tpu_custom_call" | custom-call | flops 15000000512 | bytes 1048576 | tf_op jit(solution)/shard_map/conv_own/pallas_call | solution.py:340
  30.2 0.9 %collective-permute-done.8.refs_1_ = bf16[192,768]{1,0:T(8,128)(2,1)S(1)} collective-permute-done((bf16[192,768]{1,0:T(8,128)(2,1)S(1)}, bf16[192,768]{1,0:T(8,128)(2,1)S(1)}, u32[]{:S(2)}, u32[]{:S(2)}) %collective-permute-start.8) | collective-permute-done | bytes 294944 | tf_op jit(solution)/shard_map/ppermute | solution.py:329
  31.2 0.6 %middle.3.mine_ref = bf16[384,768]{1,0:T(8,128)(2,1)S(1)} custom-call(f32[512,768]{1,0:T(8,128)S(1)} %get-tuple-element.16.own_ref, f32[768]{0:T(1024)S(1)} %copy-done.1, bf16[192,768]{1,0:T(8,128)(2,1)S(1)} %collective-permute-done.7.refs_0_, bf16[192,768]{1,0:T(8,128)(2,1)S(1)} %collective-permute-done.8.refs_1_), custom_call_target="tpu_custom_call" | custom-call | flops 50000000 | bytes 1048576 | tf_op jit(solution)/shard_map/middle/pallas_call | solution.py:364
  31.9 1.4 %collective-permute-done.5.refs_0_ = bf16[128,768]{1,0:T(8,128)(2,1)S(1)} collective-permute-done((bf16[128,768]{1,0:T(8,128)(2,1)S(1)}, bf16[128,768]{1,0:T(8,128)(2,1)S(1)}, u32[]{:S(2)}, u32[]{:S(2)}) %collective-permute-start.5) | collective-permute-done | bytes 196640 | tf_op jit(solution)/shard_map/ppermute | solution.py:329
  33.3 0.2 middle.2.mine_ref
  33.6 0.2 collective-permute-done.9.other_ref
  33.9 1.5 %final.2.refs_0_ = bf16[2,256,768]{2,1,0:T(8,128)(2,1)} custom-call(bf16[384,768]{1,0:T(8,128)(2,1)S(1)} %middle.3.mine_ref, bf16[384,768]{1,0:T(8,128)(2,1)S(1)} %collective-permute-done.9.other_ref, f32[512,768]{1,0:T(8,128)S(1)} %get-tuple-element.17.res_ref, bf16[768,768]{1,0:T(8,128)(2,1)S(1)} %get-tuple-element.18.point_ref), custom_call_target="tpu_custom_call" | custom-call | flops 500000000 | bytes 1048576 | tf_op jit(solution)/shard_map/final/pallas_call | solution.py:375
  35.4 1.0 %final.3 = bf16[2,256,768]{2,1,0:T(8,128)(2,1)} custom-call(bf16[128,768]{1,0:T(8,128)(2,1)S(1)} %middle.2.mine_ref, bf16[128,768]{1,0:T(8,128)(2,1)S(1)} %collective-permute-done.6.other_ref, f32[512,768]{1,0:T(8,128)S(1)} %get-tuple-element.17.res_ref, bf16[768,768]{1,0:T(8,128)(2,1)S(1)} %get-tuple-element.18.point_ref, ...), custom_call_target="tpu_custom_call", output_to_operand_aliasing={{}: (4, {})} | custom-call | flops 15000000512 | bytes 1048576 | tf_op jit(solution)/shard_map/final/pallas_call | solution.py:375
  (11 shorter events, 0.2 us)
Async XLA Ops:
  0.0 4.7 %collective-permute-start = (s32[1,512]{1,0:T(1,128)}, s32[1,512]{1,0:T(1,128)S(1)}, u32[]{:S(2)}, u32[]{:S(2)}) collective-permute-start(s32[1,512]{1,0:T(1,128)} %tok_any.1), channel_id=1, source_target_pairs={{0,2},{2,0},{1,3},{3,1},{4,6},{6,4},{5,7},{7,5},{8,10},{10,8},{9,1... | collective-permute-start | bytes 6152 | tf_op jit(solution)/shard_map/ppermute | solution.py:261
  3.9 13.6 %collective-permute-start.3 = (bf16[192,768]{1,0:T(8,128)(2,1)S(1)}, bf16[192,768]{1,0:T(8,128)(2,1)S(1)}, u32[]{:S(2)}, u32[]{:S(2)}) collective-permute-start(bf16[192,768]{1,0:T(8,128)(2,1)S(1)} %get-tuple-element.13), channel_id=1, source_target_pairs={{0,2},{2,0},{1,3},{3,1},{4,6},{6,4},{5,7},{7,5},{8,10},{10,8},{9,1... | collective-permute-start | bytes 884744 | tf_op jit(solution)/shard_map/ppermute | solution.py:303
  4.7 9.5 %copy-start = (f32[1536]{0:T(1024)S(1)}, f32[1536]{0:T(1024)}, u32[]{:S(2)}) copy-start(f32[1536]{0:T(1024)} %refs_3_.7) | copy-start | bytes 18436
  4.7 7.5 %collective-permute-start.1 = (s32[1,1024]{1,0:T(1,128)S(1)}, s32[1,1024]{1,0:T(1,128)S(1)}, u32[]{:S(2)}, u32[]{:S(2)}) collective-permute-start(s32[1,1024]{1,0:T(1,128)S(1)} %join.1.refs_1_), channel_id=1, source_target_pairs={{0,4},{4,8},{8,12},{1,5},{5,9},{9,13},{2,6},{6,10},{10,14},{3,7},{... | collective-permute-start | bytes 12296 | tf_op jit(solution)/shard_map/ppermute | solution.py:285
  8.7 5.5 %collective-permute-start.2 = (s32[1,1024]{1,0:T(1,128)S(1)}, s32[1,1024]{1,0:T(1,128)S(1)}, u32[]{:S(2)}, u32[]{:S(2)}) collective-permute-start(s32[1,1024]{1,0:T(1,128)S(1)} %join.1.refs_1_), channel_id=1, source_target_pairs={{4,0},{8,4},{12,8},{5,1},{9,5},{13,9},{6,2},{10,6},{14,10},{7,3},{... | collective-permute-start | bytes 12296 | tf_op jit(solution)/shard_map/ppermute | solution.py:286
  16.0 14.3 %collective-permute-start.7 = (bf16[192,768]{1,0:T(8,128)(2,1)S(1)}, bf16[192,768]{1,0:T(8,128)(2,1)S(1)}, u32[]{:S(2)}, u32[]{:S(2)}) collective-permute-start(bf16[192,768]{1,0:T(8,128)(2,1)S(1)} %conv_sent.3.refs_6_), channel_id=1, source_target_pairs={{0,2},{2,0},{1,3},{3,1},{4,6},{6,4},{5,7},{7,5},{8,10},{10,8},{9,1... | collective-permute-start | bytes 884744 | tf_op jit(solution)/shard_map/ppermute | solution.py:329
  19.3 6.8 %collective-permute-start.4 = (bf16[192,768]{1,0:T(8,128)(2,1)S(1)}, bf16[192,768]{1,0:T(8,128)(2,1)S(1)}, u32[]{:S(2)}, u32[]{:S(2)}) collective-permute-start(bf16[192,768]{1,0:T(8,128)(2,1)S(1)} %get-tuple-element.15.refs_7_), channel_id=1, source_target_pairs={{0,16},{16,0},{1,17},{17,1},{2,18},{18,2},{3,19},{19,3},{4,20},{20... | collective-permute-start | bytes 884744 | tf_op jit(solution)/shard_map/ppermute | solution.py:336
  20.9 10.3 %collective-permute-start.8 = (bf16[192,768]{1,0:T(8,128)(2,1)S(1)}, bf16[192,768]{1,0:T(8,128)(2,1)S(1)}, u32[]{:S(2)}, u32[]{:S(2)}) collective-permute-start(bf16[192,768]{1,0:T(8,128)(2,1)S(1)} %get-tuple-element.14.refs_5_), channel_id=1, source_target_pairs={{0,2},{2,0},{1,3},{3,1},{4,6},{6,4},{5,7},{7,5},{8,10},{10,8},{9,1... | collective-permute-start | bytes 884744 | tf_op jit(solution)/shard_map/ppermute | solution.py:329
  23.1 8.1 %copy-start.1 = (f32[768]{0:T(1024)S(1)}, f32[768]{0:T(1024)}, u32[]{:S(2)}) copy-start(f32[768]{0:T(1024)} %gain_ref.3) | copy-start | bytes 9220
  23.1 10.2 %collective-permute-start.5 = (bf16[128,768]{1,0:T(8,128)(2,1)S(1)}, bf16[128,768]{1,0:T(8,128)(2,1)S(1)}, u32[]{:S(2)}, u32[]{:S(2)}) collective-permute-start(bf16[128,768]{1,0:T(8,128)(2,1)S(1)} %conv_sent.5.refs_5_), channel_id=1, source_target_pairs={{0,2},{2,0},{1,3},{3,1},{4,6},{6,4},{5,7},{7,5},{8,10},{10,8},{9,1... | collective-permute-start | bytes 589832 | tf_op jit(solution)/shard_map/ppermute | solution.py:329
  31.8 2.1 %collective-permute-start.9 = (bf16[384,768]{1,0:T(8,128)(2,1)S(1)}, bf16[384,768]{1,0:T(8,128)(2,1)S(1)}, u32[]{:S(2)}, u32[]{:S(2)}) collective-permute-start(bf16[384,768]{1,0:T(8,128)(2,1)S(1)} %middle.3.mine_ref), channel_id=1, source_target_pairs={{0,1},{1,0},{2,3},{3,2},{4,5},{5,4},{6,7},{7,6},{8,9},{9,8},{10,11... | collective-permute-start | bytes 1769480 | tf_op jit(solution)/shard_map/ppermute | solution.py:373
  33.6 1.8 %collective-permute-start.6 = (bf16[128,768]{1,0:T(8,128)(2,1)S(1)}, bf16[128,768]{1,0:T(8,128)(2,1)S(1)}, u32[]{:S(2)}, u32[]{:S(2)}) collective-permute-start(bf16[128,768]{1,0:T(8,128)(2,1)S(1)} %middle.2.mine_ref), channel_id=1, source_target_pairs={{0,1},{1,0},{2,3},{3,2},{4,5},{5,4},{6,7},{7,6},{8,9},{9,8},{10,11... | collective-permute-start | bytes 589832 | tf_op jit(solution)/shard_map/ppermute | solution.py:373
